TPU v7x, 512 devices: a whole 4x4x16 slice. The times are simulated.
512 devices in a mesh: ctx: 16 (over x, y), exp: 32 (over z, core).
Axes of the slice: x: 4, y: 4, z: 16, core: 2. Of those that a mesh axis runs over, the one named last changes fastest.
Arguments:
- resid: bfloat16 [2048, 3072], P('ctx', 'exp'), may hold values from -37 to 37
- queries: bfloat16 [2048, 4096], P('ctx', 'exp'), may hold values from -6 to 6
- keys: bfloat16 [2048, 4096], P('ctx', 'exp'), may hold values from -0.01171875 to 0.01171875
- values: bfloat16 [2048, 4096], P('ctx', 'exp'), may hold values from -6 to 6
- log_decay: float32 [32, 2048], P('exp', 'ctx'), may hold values from -1.5 to 0
- w_out: bfloat16 [4096, 3072], P('exp'), may hold values from -0.1875 to 0.1875
- w_up: bfloat16 [32, 3072, 6144], P('exp', None, 'ctx'), may hold values from -0.07307089 to 0.07307089
- w_down: bfloat16 [32, 6144, 3072], P('exp', 'ctx'), may hold values from -0.076546554 to 0.076546554
- expert_ids: int32 [2048, 2], P('ctx'), may hold values from 0 to 31, all different within a row; in each aligned block of 128 rows (0 to 127, 128 to 255, ...) at most 16 rows name the same one
- route_weights: float32 [2048, 2], P('ctx'), may hold values from 0.3 to 1.5
- cotangent: bfloat16 [2048, 3072], P('ctx', 'exp'), may hold values from -6 to 6
Outputs:
- layer_out: bfloat16 [2048, 3072], P('ctx', 'exp')
- resid_grad: bfloat16 [2048, 3072], P('ctx', 'exp')
- q_grad: bfloat16 [2048, 4096], P('ctx', 'exp')
- k_grad: bfloat16 [2048, 4096], P('ctx', 'exp')
- v_grad: bfloat16 [2048, 4096], P('ctx', 'exp')
Inputs may be any that keep to these rules, and one draw needn't show every extreme that they name: `expert_ids`: in each aligned block of 128 rows (the positions of one block) no expert is named by more than 16 rows; the two ids of a row differ.
All inputs are finite; a program needn't handle non-finite values.
Results may differ from a plain program's by a relative error of at most 0.02.
Values may be sent and summed in bfloat16 or wider, within the bound.
No kernel may reach another device: no remote copies, remote signals or barrier semaphores. Data moves between devices by JAX's collectives and lax.ppermute only.
A program may use at most 64 MiB of HBM per device.

v0:
```python
import jax
import jax.numpy as jnp
from jax import lax
from jax.sharding import PartitionSpec as P

highest_score = lax.Precision.HIGHEST


def prefix(shard, axis, join, neutral, backward):
    count = lax.axis_size(axis)
    place = lax.axis_index(axis)
    ahead = count - 1 - place if backward else place
    gathered = jax.tree.map(
        lambda a, kind: lax.all_gather(a.astype(kind), axis), shard, (jnp.bfloat16, jnp.bfloat16)
    )
    state = jax.tree.map(lambda a, e: jnp.zeros_like(a) + jnp.asarray(e, a.dtype), shard, neutral)

    def one(hop, state):
        source = count - 1 - hop if backward else hop
        return join(
            state,
            jax.tree.map(
                lambda a, own: lax.dynamic_index_in_dim(a, source, 0, False).astype(own.dtype),
                gathered,
                shard,
            ),
        )

    return lax.fori_loop(0, ahead, one, state)


def block_decays(decay_rows):
    cum = jnp.cumsum(decay_rows, axis=-1)
    last = cum[:, -1]
    token_offset = jnp.arange(decay_rows.shape[-1])
    causal = token_offset[:, None] >= token_offset[None, :]
    gaps = jnp.where(causal[None], cum[:, :, None] - cum[:, None, :], -jnp.inf)
    return (cum, last, jnp.exp(gaps))


def silu_grad(upper):
    sigma = jax.nn.sigmoid(upper)
    return sigma * (1.0 + upper * (1.0 - sigma))


def split_heads(matrix, head_count):
    tokens_here = matrix.shape[0]
    return matrix.astype(jnp.float32).reshape(tokens_here, head_count, -1).transpose(1, 0, 2)


def join_heads(blocks):
    return blocks.transpose(1, 0, 2).reshape(blocks.shape[1], -1).astype(jnp.bfloat16)


def local(
    resid,
    queries,
    keys,
    values,
    log_decay,
    w_out,
    w_up,
    w_down,
    expert_ids,
    route_weights,
    cotangent,
):
    head_count = log_decay.shape[0]
    tokens_here = queries.shape[0]
    query_heads = split_heads(queries, head_count)
    head_keys = split_heads(keys, head_count)
    head_values = split_heads(values, head_count)
    cum, last, decay_matrix = block_decays(log_decay)
    keep_mask = jnp.exp(last[:, None] - cum)[..., None]
    router_scores = (
        jnp.einsum("htd,hid->hti", query_heads, head_keys, precision=highest_score) * decay_matrix
    )
    local_state = jnp.einsum(
        "hid,hie->hde", head_keys * keep_mask, head_values, precision=highest_score
    )

    def link(early, later):
        return (early[0] + later[0], jnp.exp(later[0])[:, None, None] * early[1] + later[1])

    blank = (jnp.zeros_like(last), jnp.zeros_like(local_state))
    _, incoming = prefix((last, local_state), "ctx", link, blank, False)
    inner = jnp.einsum("hti,hid->htd", router_scores, head_values, precision=highest_score)
    outer = jnp.exp(cum)[..., None] * jnp.einsum(
        "htd,hde->hte", query_heads, incoming, precision=highest_score
    )
    attn_heads = join_heads(inner + outer)
    width = w_out.shape[1]
    share = width // lax.axis_size("exp")
    columns = w_out
    attn = (
        lax.psum_scatter(
            lax.dot_general(
                columns, attn_heads, (((0,), (1,)), ((), ())), preferred_element_type=jnp.float32
            ).astype(jnp.bfloat16),
            "exp",
            scatter_dimension=0,
            tiled=True,
        )
        .astype(jnp.float32)
        .T.astype(jnp.bfloat16)
    )
    residual = (resid.astype(jnp.float32) + attn.astype(jnp.float32)).astype(jnp.bfloat16)
    residual_f = residual.astype(jnp.float32)
    square_sum = lax.psum(jnp.sum(residual_f * residual_f, axis=1), "exp")
    rstd = lax.rsqrt(square_sum / width + 1e-06)
    normed = (residual_f * rstd[:, None]).astype(jnp.bfloat16)
    expert_count = w_up.shape[0] * lax.axis_size("exp")
    capacity = 4 * tokens_here // expert_count
    onehot = (expert_ids[:, :, None] == jnp.arange(expert_count)[None, None, :]).astype(jnp.int32)
    flat = onehot.reshape(tokens_here * 2, expert_count)
    before = jnp.cumsum(flat, axis=0) - flat
    slots = jnp.sum(before * flat, axis=1).reshape(tokens_here, 2)
    position = expert_ids * capacity + slots
    place = position[:, :, None] == jnp.arange(expert_count * capacity)[None, None, :]
    picks = place.astype(jnp.bfloat16)
    placed = jnp.sum(place.astype(jnp.int32), axis=1).astype(jnp.bfloat16)
    sent_rows = lax.dot_general(
        placed, normed, (((0,), (0,)), ((), ())), preferred_element_type=jnp.float32
    )
    sent_rows = sent_rows.astype(jnp.bfloat16).reshape(expert_count, capacity, share)
    expert_in = lax.all_to_all(sent_rows, "exp", split_axis=0, concat_axis=2, tiled=True)
    all_rows = lax.all_gather(expert_in, "ctx", axis=1, tiled=True)
    upper = jnp.einsum("erd,edf->erf", all_rows, w_up, preferred_element_type=jnp.float32)
    act = jax.nn.silu(upper).astype(jnp.bfloat16)
    partial_out = jnp.einsum("erf,efd->erd", act, w_down, preferred_element_type=jnp.float32)
    expert_out = lax.psum_scatter(
        partial_out.astype(jnp.bfloat16), "ctx", scatter_dimension=1, tiled=True
    )
    returned = lax.all_to_all(expert_out, "exp", split_axis=2, concat_axis=0, tiled=True).reshape(
        expert_count * capacity, share
    )
    routed = jnp.einsum("tks,sd->tkd", picks, returned, preferred_element_type=jnp.float32)
    layer_out = (residual_f + jnp.sum(route_weights[:, :, None] * routed, axis=1)).astype(
        jnp.bfloat16
    )
    cot_f = cotangent.astype(jnp.float32)
    slot_weight = jnp.einsum(
        "tks,tk->s", place.astype(jnp.float32), route_weights, precision=highest_score
    )
    grad_rows_local = lax.dot_general(
        placed, cotangent, (((0,), (0,)), ((), ())), preferred_element_type=jnp.float32
    )
    grad_send = (
        (grad_rows_local * slot_weight[:, None])
        .astype(jnp.bfloat16)
        .reshape(expert_count, capacity, share)
    )
    grad_in = lax.all_to_all(grad_send, "exp", split_axis=0, concat_axis=2, tiled=True)
    grad_all = lax.all_gather(grad_in, "ctx", axis=1, tiled=True)
    grad_act = jnp.einsum("erd,efd->erf", grad_all, w_down, preferred_element_type=jnp.float32)
    grad_up = (grad_act * silu_grad(upper)).astype(jnp.bfloat16)
    partial_grad = jnp.einsum("erf,edf->erd", grad_up, w_up, preferred_element_type=jnp.float32)
    grad_expert = lax.psum_scatter(
        partial_grad.astype(jnp.bfloat16), "ctx", scatter_dimension=1, tiled=True
    )
    grad_back = lax.all_to_all(grad_expert, "exp", split_axis=2, concat_axis=0, tiled=True).reshape(
        expert_count * capacity, share
    )
    grad_normed = jnp.dot(placed, grad_back, preferred_element_type=jnp.float32)
    inner_dot = lax.psum(jnp.sum(grad_normed * residual_f, axis=1), "exp")
    grad_resid = (
        rstd[:, None] * grad_normed - residual_f * (rstd * rstd * rstd * inner_dot / width)[:, None]
    )
    resid_grad = (cot_f + grad_resid).astype(jnp.bfloat16)
    columns = w_out
    grad_flat = lax.dot_general(
        lax.all_gather(resid_grad, "exp", axis=1, tiled=True),
        columns,
        (((1,), (1,)), ((), ())),
        preferred_element_type=jnp.float32,
    )
    head_gradient = split_heads(grad_flat, head_count)
    local_grad = jnp.einsum(
        "hta,htb->hab",
        query_heads * jnp.exp(cum)[..., None],
        head_gradient,
        precision=highest_score,
    )

    def back_link(early, later):
        return (early[0] + later[0], later[1] + jnp.exp(later[0])[:, None, None] * early[1])

    blank_grad = (jnp.zeros_like(last), jnp.zeros_like(local_grad))
    _, carried_state = prefix((last, local_grad), "ctx", back_link, blank_grad, True)
    score_gradient = (
        jnp.einsum("coy,cwy->cow", head_gradient, head_values, precision=highest_score)
        * decay_matrix
    )
    query_grad = jnp.einsum("hti,hia->hta", score_gradient, head_keys, precision=highest_score)
    query_grad = query_grad + jnp.exp(cum)[..., None] * jnp.einsum(
        "htb,hab->hta", head_gradient, incoming, precision=highest_score
    )
    key_gradient = jnp.einsum("hti,hta->hia", score_gradient, query_heads, precision=highest_score)
    key_gradient = key_gradient + keep_mask * jnp.einsum(
        "qsv,qnv->qsn", head_values, carried_state, precision=highest_score
    )
    value_gradient = jnp.einsum(
        "nyw,nyx->nwx", router_scores, head_gradient, precision=highest_score
    )
    value_gradient = value_gradient + keep_mask * jnp.einsum(
        "sfc,scl->sfl", head_keys, carried_state, precision=highest_score
    )
    return (
        layer_out,
        resid_grad,
        join_heads(query_grad),
        join_heads(key_gradient),
        join_heads(value_gradient),
    )


def solution(mesh):
    return jax.shard_map(
        local,
        mesh=mesh,
        in_specs=(
            P("ctx", "exp"),
            P("ctx", "exp"),
            P("ctx", "exp"),
            P("ctx", "exp"),
            P("exp", "ctx"),
            P("exp", None),
            P("exp", None, "ctx"),
            P("exp", "ctx", None),
            P("ctx", None),
            P("ctx", None),
            P("ctx", "exp"),
        ),
        out_specs=(
            P("ctx", "exp"),
            P("ctx", "exp"),
            P("ctx", "exp"),
            P("ctx", "exp"),
            P("ctx", "exp"),
        ),
        check_vma=False,
    )
```

profile of v0, /device:TPU:32, one launch (start us, length us, event | category | flops | bytes accessed | tf_op | source)
XLA Modules:
  0.0 780.2 jit_solution(4295536002061562439)
XLA Ops:
  7.3 1.1 reduce_window_sum.26
  9.6 0.7 bitcast_exponential_fusion
  10.3 1.3 dynamic-slice
  11.6 1.1 convolution_convert_fusion.5
  12.7 0.8 dynamic-update-slice
  13.5 26.2 %all-gather = bf16[2048,128]{1,0:T(8,128)(2,1)} all-gather(bf16[128,128]{1,0:T(8,128)(2,1)S(1)} %convolution_convert_fusion.5), channel_id=2, replica_groups=mesh['ctx'=16,'exp'=32] {'ctx'}, dimensions={0}, use_global_device_ids=true | all-gather | bytes 557056 | tf_op jit(solution)/shard_map/all_gather | solution.py:14
  39.7 38.1 %all-reduce = bf16[16]{0:T(256)(128)(2,1)S(1)} all-reduce(bf16[16]{0:T(256)(128)(2,1)S(1)} %dynamic-update-slice), channel_id=1, replica_groups=mesh['ctx'=16,'exp'=32] {'ctx'}, use_global_device_ids=true, to_apply=%add | all-reduce | flops 16 | bytes 64
  78.9 1.3 fusion.2
  80.2 2.3 copy.121
  83.0 0.6 reduce-window.6
  84.2 131.8 %reduce-scatter.10.cloned.1.call-done = bf16[96,128]{1,0:T(8,128)(2,1)} async-done(((bf16[3072,128]{1,0:T(8,128)(2,1)}), bf16[96,128]{1,0:T(8,128)(2,1)}) %reduce-scatter.10.cloned.1.call-update) | async-done | bytes 24592 | tf_op jit(solution)/shard_map/reduce_scatter | solution.py:96
  216.1 0.8 fusion.55
  216.8 45.9 %psum.14 = f32[128]{0:T(128)S(1)} all-reduce(f32[128]{0:T(128)S(1)} %get-tuple-element.215), channel_id=1, replica_groups=mesh['ctx'=16,'exp'=32] {'exp'}, use_global_device_ids=true, to_apply=%region_9.10 | all-reduce | flops 128 | bytes 1024 | tf_op jit(solution)/shard_map/psum | solution.py:109
  263.1 30.3 %all_to_all.66 = bf16[32,16,96]{2,1,0:T(8,128)(2,1)S(1)} all-to-all(bf16[32,16,96]{2,1,0:T(8,128)(2,1)S(1)} %bitcast.175), channel_id=1, replica_groups=mesh['ctx'=16,'exp'=32] {'exp'}, dimensions={0} | all-to-all | bytes 196608 | tf_op jit(solution)/shard_map/all_to_all | solution.py:126
  293.5 0.8 all_to_all.51
  295.0 20.5 %all_to_all.67 = bf16[32,16,96]{2,1,0:T(8,128)(2,1)S(1)} all-to-all(bf16[32,16,96]{2,1,0:T(8,128)(2,1)S(1)} %bitcast.176), channel_id=1, replica_groups=mesh['ctx'=16,'exp'=32] {'exp'}, dimensions={0} | all-to-all | bytes 196608 | tf_op jit(solution)/shard_map/all_to_all | solution.py:153
  315.5 0.8 all_to_all.58
  316.4 29.6 %all-gather.5.cloned.1.call-done = bf16[1,256,3072]{2,1,0:T(8,128)(2,1)} async-done(((bf16[1,16,3072]{2,1,0:T(8,128)(2,1)}), bf16[1,256,3072]{2,1,0:T(8,128)(2,1)}) %all-gather.5.cloned.1.call-update) | async-done | bytes 1572880 | tf_op jit(solution)/shard_map/all_gather | solution.py:127
  346.0 3.1 fusion.7
  349.1 59.1 %all-gather.7.cloned.1.call-done = bf16[1,256,3072]{2,1,0:T(8,128)(2,1)} async-done(((bf16[1,16,3072]{2,1,0:T(8,128)(2,1)}), bf16[1,256,3072]{2,1,0:T(8,128)(2,1)}) %all-gather.7.cloned.1.call-update) | async-done | bytes 1572880 | tf_op jit(solution)/shard_map/all_gather | solution.py:154
  408.2 5.2 fusion.1
  413.7 2.2 fusion
  415.9 86.2 %reduce-scatter.8.cloned.1.call-done = bf16[1,16,3072]{2,1,0:T(8,128)(2,1)} async-done(((bf16[1,256,3072]{2,1,0:T(8,128)(2,1)}), bf16[1,16,3072]{2,1,0:T(8,128)(2,1)}) %reduce-scatter.8.cloned.1.call-update) | async-done | bytes 98320 | tf_op jit(solution)/shard_map/reduce_scatter | solution.py:158
  502.1 3.6 copy.109
  506.2 18.0 %reduce.2 = bf16[3072,16]{1,0:T(8,128)(2,1)S(1)} reduce(bf16[3072,1,16]{2,1,0:T(2,128)(2,1)} %bitcast.168, bf16[]{:T(256)} %broadcast.70), dimensions={1}, to_apply=%bitcast.130.reduce_sub_computation | reduce | bytes 196610
  524.2 1.3 reshape.274
  525.5 12.9 %all-to-all-start.3 = ((bf16[32,2,768]{2,1,0:T(2,128)(2,1)}), bf16[32,2,768]{2,1,0:T(2,128)(2,1)}, u32[]{:S(2)}, u32[]{:S(2)}) async-start(bf16[32,2,768]{2,1,0:T(2,128)(2,1)} %reshape.274), calls=%async_computation.5 | async-start | bytes 196608 | tf_op jit(solution)/shard_map/all_to_all | solution.py:161
  538.3 56.6 %reduce-scatter.6.cloned.1.call-done = bf16[1,16,3072]{2,1,0:T(8,128)(2,1)} async-done(((bf16[1,256,3072]{2,1,0:T(8,128)(2,1)}), bf16[1,16,3072]{2,1,0:T(8,128)(2,1)}) %reduce-scatter.6.cloned.1.call-update) | async-done | bytes 98320 | tf_op jit(solution)/shard_map/reduce_scatter | solution.py:131
  595.0 3.6 copy.103
  598.6 18.0 %reduce.3 = bf16[3072,16]{1,0:T(8,128)(2,1)S(1)} reduce(bf16[3072,1,16]{2,1,0:T(2,128)(2,1)} %bitcast.169, bf16[]{:T(256)} %broadcast.70), dimensions={1}, to_apply=%bitcast.128.reduce_sub_computation | reduce | bytes 196610
  616.6 1.3 reshape.272
  617.9 12.8 %all-to-all-start.1 = ((bf16[32,2,768]{2,1,0:T(2,128)(2,1)}), bf16[32,2,768]{2,1,0:T(2,128)(2,1)S(1)}, u32[]{:S(2)}, u32[]{:S(2)}) async-start(bf16[32,2,768]{2,1,0:T(2,128)(2,1)} %reshape.272), calls=%async_computation.2 | async-start | bytes 196608 | tf_op jit(solution)/shard_map/all_to_all | solution.py:134
  630.7 4.9 reshape.275
  635.6 3.3 copy.110
  639.4 45.4 %psum.15 = f32[128]{0:T(128)S(1)} all-reduce(f32[128]{0:T(128)S(1)} %get-tuple-element.221), channel_id=1, replica_groups=mesh['ctx'=16,'exp'=32] {'exp'}, use_global_device_ids=true, to_apply=%region_14.15 | all-reduce | flops 128 | bytes 1024 | tf_op jit(solution)/shard_map/psum | solution.py:165
  685.3 2.4 reshape.273
  687.8 3.4 copy.104
  691.5 1.0 fusion.22
  692.5 1.4 fusion.61
  693.9 33.0 %all_gather.32 = bf16[128,3072]{0,1:T(8,128)(2,1)S(1)} all-gather(bf16[128,96]{0,1:T(8,128)(2,1)S(1)} %get-tuple-element.217), channel_id=1, replica_groups=mesh['ctx'=16,'exp'=32] {'exp'}, dimensions={1}, use_global_device_ids=true | all-gather | bytes 811008 | tf_op jit(solution)/shard_map/all_gather | solution.py:172
  728.6 23.3 %all-gather.1 = bf16[2048,128]{1,0:T(8,128)(2,1)S(1)} all-gather(bf16[128,128]{1,0:T(8,128)(2,1)S(1)} %convolution_convert_fusion.4), channel_id=3, replica_groups=mesh['ctx'=16,'exp'=32] {'ctx'}, dimensions={0}, use_global_device_ids=true | all-gather | bytes 557056 | tf_op jit(solution)/shard_map/all_gather | solution.py:14
  751.9 19.2 %while.27 = (s32[]{:T(128)}, f32[1,128,128]{2,1,0:T(8,128)S(1)}, s32[]{:T(128)}, bf16[16,1,128,128]{3,2,1,0:T(8,128)(2,1)S(1)}, bf16[16,1]{0,1:T(2,128)(2,1)S(1)...) while((s32[]{:T(128)}, f32[1,128,128]{2,1,0:T(8,128)S(1)}, s32[]{:T(128)}, ...), condition=%wide.region_16.17_spmd, body=%wide.region_15.16_spmd.sunk | while | flops 49158 | bytes 163997 | solution.py:29
  752.0 0.6 fusion.116
  752.5 0.7 convert_add_fusion.6
  753.2 0.6 fusion.116
  753.8 0.7 convert_add_fusion.6
  754.5 0.6 fusion.116
  755.1 0.7 convert_add_fusion.6
  755.8 0.6 fusion.116
  756.4 0.7 convert_add_fusion.6
  757.7 0.7 convert_add_fusion.6
  759.0 0.7 convert_add_fusion.6
  760.2 0.7 convert_add_fusion.6
  761.5 0.7 convert_add_fusion.6
  762.8 0.7 convert_add_fusion.6
  764.1 0.7 convert_add_fusion.6
  765.4 0.7 convert_add_fusion.6
  766.6 0.7 convert_add_fusion.6
  767.9 0.7 convert_add_fusion.6
  769.2 0.7 convert_add_fusion.6
  770.5 0.7 convert_add_fusion.6
  771.2 0.8 fusion.33
  772.0 0.8 fusion.32
  772.8 0.9 fusion.31
  (114 shorter events, 14.1 us)
Async XLA Ops:
  7.2 401.1 %copy-start = (bf16[1,384,3072]{2,1,0:T(8,128)(2,1)S(1)}, bf16[1,384,3072]{2,1,0:T(8,128)(2,1)}, u32[]{:S(2)}) copy-start(bf16[1,384,3072]{2,1,0:T(8,128)(2,1)} %param.22) | copy-start | bytes 7077892
  7.2 70.7 %copy-start.5 = (bf16[128,128]{1,0:T(8,128)(2,1)S(1)}, bf16[128,128]{1,0:T(8,128)(2,1)}, u32[]{:S(2)}) copy-start(bf16[128,128]{1,0:T(8,128)(2,1)} %param.17) | copy-start | bytes 98308
  7.2 70.9 %copy-start.3 = (bf16[128,128]{1,0:T(8,128)(2,1)S(1)}, bf16[128,128]{1,0:T(8,128)(2,1)}, u32[]{:S(2)}) copy-start(bf16[128,128]{1,0:T(8,128)(2,1)} %param.18) | copy-start | bytes 98308
  7.2 70.7 %copy-start.7 = (bf16[128,128]{1,0:T(8,128)(2,1)S(1)}, bf16[128,128]{1,0:T(8,128)(2,1)}, u32[]{:S(2)}) copy-start(bf16[128,128]{1,0:T(8,128)(2,1)} %param.16) | copy-start | bytes 98308
  7.2 71.6 %copy-start.1 = (bf16[128,3072]{1,0:T(8,128)(2,1)S(1)}, bf16[128,3072]{1,0:T(8,128)(2,1)}, u32[]{:S(2)}) copy-start(bf16[128,3072]{1,0:T(8,128)(2,1)} %param.20) | copy-start | bytes 2359300
  7.2 208.8 %reduce-scatter.10.cloned.1.call-start = ((), (), s32[]{:S(2)}) async-start(), calls=%async_computation.11 | async-start | bytes 811008 | tf_op jit(solution)/shard_map/reduce_scatter | solution.py:96
  8.4 71.8 %copy-start.18 = (f32[1,128]{1,0:T(1,128)}, f32[1,128]{1,0:T(1,128)S(1)}, u32[]{:S(2)}) copy-start(f32[1,128]{1,0:T(1,128)S(1)} %reduce_window_sum.26) | copy-start | bytes 1540
  10.3 67.5 %copy-start.16 = (f32[128]{0:T(128)}, f32[128]{0:T(128)S(1)}, u32[]{:S(2)}) copy-start(f32[128]{0:T(128)S(1)} %get-tuple-element.220) | copy-start | bytes 1540
  10.3 69.8 %copy-start.14 = (f32[128]{0:T(128)}, f32[128]{0:T(128)S(1)}, u32[]{:S(2)}) copy-start(f32[128]{0:T(128)S(1)} %get-tuple-element.219) | copy-start | bytes 1540
  77.9 4.6 copy-start.23
  78.1 0.6 copy-start.9
  80.1 2.4 copy-start.20
  80.1 135.9 %copy-start.13 = (bf16[128,96]{0,1:T(8,128)(2,1)S(1)}, bf16[128,96]{0,1:T(8,128)(2,1)}, u32[]{:S(2)}) copy-start(bf16[128,96]{0,1:T(8,128)(2,1)} %param.15) | copy-start | bytes 73732
  82.5 211.9 %copy-start.22 = (f32[128,2]{0,1:T(2,128)S(1)}, f32[128,2]{0,1:T(2,128)}, u32[]{:S(2)}) copy-start(f32[128,2]{0,1:T(2,128)} %param.24) | copy-start | bytes 3076
  82.5 212.2 %copy-start.12 = (bf16[128,96]{0,1:T(8,128)(2,1)S(1)}, bf16[128,96]{0,1:T(8,128)(2,1)}, u32[]{:S(2)}) copy-start(bf16[128,96]{0,1:T(8,128)(2,1)} %param.25) | copy-start | bytes 73732
  82.5 263.5 %all-gather.5.cloned.1.call-start = ((), (), s32[]{:S(2)}) async-start(), calls=%async_computation.7 | async-start | bytes 1671168 | tf_op jit(solution)/shard_map/all_gather | solution.py:127
  262.8 31.6 %copy-start.21 = (f32[128]{0:T(128)}, f32[128]{0:T(128)S(1)}, u32[]{:S(2)}) copy-start(f32[128]{0:T(128)S(1)} %add_rsqrt_fusion) | copy-start | bytes 1540
  294.3 113.9 %all-gather.7.cloned.1.call-start = ((), (), s32[]{:S(2)}) async-start(), calls=%async_computation.9 | async-start | bytes 1671168 | tf_op jit(solution)/shard_map/all_gather | solution.py:154
  316.4 185.7 %reduce-scatter.8.cloned.1.call-start = ((), (), s32[]{:S(2)}) async-start(), calls=%async_computation.10 | async-start | bytes 1671168 | tf_op jit(solution)/shard_map/reduce_scatter | solution.py:158
  413.5 181.5 %reduce-scatter.6.cloned.1.call-start = ((), (), s32[]{:S(2)}) async-start(), calls=%async_computation.8 | async-start | bytes 1671168 | tf_op jit(solution)/shard_map/reduce_scatter | solution.py:131
  525.5 92.4 %all-to-all-start.3 = ((bf16[32,2,768]{2,1,0:T(2,128)(2,1)}), bf16[32,2,768]{2,1,0:T(2,128)(2,1)}, u32[]{:S(2)}, u32[]{:S(2)}) async-start(bf16[32,2,768]{2,1,0:T(2,128)(2,1)} %reshape.274), calls=%async_computation.5 | async-start | bytes 196608 | tf_op jit(solution)/shard_map/all_to_all | solution.py:161
  617.9 67.5 %all-to-all-start.1 = ((bf16[32,2,768]{2,1,0:T(2,128)(2,1)}), bf16[32,2,768]{2,1,0:T(2,128)(2,1)S(1)}, u32[]{:S(2)}, u32[]{:S(2)}) async-start(bf16[32,2,768]{2,1,0:T(2,128)(2,1)} %reshape.272), calls=%async_computation.2 | async-start | bytes 196608 | tf_op jit(solution)/shard_map/all_to_all | solution.py:134
  687.7 39.1 %copy-start.2 = (bf16[128,3072]{1,0:T(8,128)(2,1)S(1)}, bf16[128,3072]{1,0:T(8,128)(2,1)}, u32[]{:S(2)}) copy-start(bf16[128,3072]{1,0:T(8,128)(2,1)} %param.20) | copy-start | bytes 2359300
  691.3 35.9 %copy-start.8 = (bf16[128,128]{1,0:T(8,128)(2,1)S(1)}, bf16[128,128]{1,0:T(8,128)(2,1)}, u32[]{:S(2)}) copy-start(bf16[128,128]{1,0:T(8,128)(2,1)} %param.16) | copy-start | bytes 98308
  691.4 35.9 %copy-start.15 = (f32[128]{0:T(128)S(1)}, f32[128]{0:T(128)}, u32[]{:S(2)}) copy-start(f32[128]{0:T(128)} %copy-done.14) | copy-start | bytes 1540
  691.4 36.2 %copy-start.10 = (f32[128,128]{1,0:T(8,128)S(1)}, f32[128,128]{1,0:T(8,128)}, u32[]{:S(2)}) copy-start(f32[128,128]{1,0:T(8,128)} %copy-done.9) | copy-start | bytes 196612
  691.4 36.5 %copy-start.4 = (bf16[128,128]{1,0:T(8,128)(2,1)S(1)}, bf16[128,128]{1,0:T(8,128)(2,1)}, u32[]{:S(2)}) copy-start(bf16[128,128]{1,0:T(8,128)(2,1)} %param.18) | copy-start | bytes 98308
  691.4 36.5 %copy-start.19 = (f32[1,128]{1,0:T(1,128)S(1)}, f32[1,128]{1,0:T(1,128)}, u32[]{:S(2)}) copy-start(f32[1,128]{1,0:T(1,128)} %copy-done.18) | copy-start | bytes 1540
  693.9 34.8 %copy-start.11 = (bf16[128,96]{0,1:T(8,128)(2,1)}, bf16[128,96]{0,1:T(8,128)(2,1)S(1)}, u32[]{:S(2)}) copy-start(bf16[128,96]{0,1:T(8,128)(2,1)S(1)} %get-tuple-element.217) | copy-start | bytes 73732
  693.9 34.6 %copy-start.6 = (bf16[128,128]{1,0:T(8,128)(2,1)S(1)}, bf16[128,128]{1,0:T(8,128)(2,1)}, u32[]{:S(2)}) copy-start(bf16[128,128]{1,0:T(8,128)(2,1)} %param.17) | copy-start | bytes 98308
  726.9 25.1 %copy-start.24 = (bf16[16,1]{0,1:T(2,128)(2,1)S(1)}, bf16[16,1]{0,1:T(2,128)(2,1)}, u32[]{:S(2)}) copy-start(bf16[16,1]{0,1:T(2,128)(2,1)} %copy-done.23) | copy-start | bytes 100
  727.3 43.9 %copy-start.17 = (f32[128]{0:T(128)S(1)}, f32[128]{0:T(128)}, u32[]{:S(2)}) copy-start(f32[128]{0:T(128)} %copy-done.16) | copy-start | bytes 1540
Sparse Core Ops, SparseCore 0:
  82.6 133.4 reduce-scatter.9
  294.4 51.4 all-gather.4
  349.5 58.7 all-gather.6
  413.6 88.4 reduce-scatter.7
  506.6 88.3 reduce-scatter.5
where the time goes:
time: 783 us; the launch traced here: 780 us
  waiting for transfers between devices  363 us (46%)
  blocking collectives  263 us (34%)
  other arithmetic  51.2 us (7%)
  local copies, waits for them, and re-layouts  41.8 us (5%)
  starting transfers between devices  26.1 us (3%)
  matrix products  19.5 us (2%)
  between operations  15 us (2%)
    reduce_scatter x1, waiting for transfers between devices, local(): lax.psum_scatter(lax.dot_general(columns, attn_heads, (((0,), (1,)), ((),...  132 us
    reduce_scatter x1, waiting for transfers between devices, local(): lax.psum_scatter(partial_grad.astype(jnp.bfloat16), 'ctx', scatter_dimens...  86.2 us
    all_gather x1, waiting for transfers between devices, local(): grad_all = lax.all_gather(grad_in, 'ctx', axis=1, tiled=True)  59.1 us
    reduce_scatter x1, waiting for transfers between devices, local(): lax.psum_scatter(partial_out.astype(jnp.bfloat16), 'ctx', scatter_dimensi...  56.6 us
    all_gather x2, blocking collectives, prefix(): lax.all_gather(a.astype(kind), axis)  49.5 us
    psum x1, blocking collectives, local(): square_sum = lax.psum(jnp.sum(residual_f * residual_f, axis=1), 'exp')  45.9 us
    psum x1, blocking collectives, local(): inner_dot = lax.psum(jnp.sum(grad_normed * residual_f, axis=1), 'exp')  45.4 us
    unnamed x1, blocking collectives  38.1 us
  transfers between devices with their start and end apart: 7, of which 5 were waited for; matrix products, arithmetic and copies ran while one was open for 8% of the time, Pallas kernels for 0%

commit v1 on v0

--- a/solution.py
+++ b/solution.py
@@ -4,6 +4,12 @@
 from jax.sharding import PartitionSpec as P
 
 highest_score = lax.Precision.HIGHEST
+
+
+def joined_along(tiles, dim):
+    tiles = jnp.moveaxis(tiles, 0, dim)
+    dims = tiles.shape
+    return tiles.reshape(*dims[:dim], dims[dim] * dims[dim + 1], *dims[dim + 2 :])
 
 
 def prefix(shard, axis, join, neutral, backward):
@@ -151,8 +157,16 @@
         .reshape(expert_count, capacity, share)
     )
     grad_in = lax.all_to_all(grad_send, "exp", split_axis=0, concat_axis=2, tiled=True)
-    grad_all = lax.all_gather(grad_in, "ctx", axis=1, tiled=True)
-    grad_act = jnp.einsum("erd,efd->erf", grad_all, w_down, preferred_element_type=jnp.float32)
+    peers, here, rows = (lax.axis_size("ctx"), lax.axis_index("ctx"), grad_in.shape[1])
+    ahead_2 = [(i, (i + 1) % peers) for i in range(peers)]
+    parts = []
+    held = grad_in
+    for hop_2 in range(peers):
+        coming = held if hop_2 == peers - 1 else lax.ppermute(held, "ctx", ahead_2)
+        parts.append(jnp.einsum("erd,efd->erf", held, w_down, preferred_element_type=jnp.float32))
+        held = coming
+    parts = jnp.stack(parts)[(here - jnp.arange(peers)) % peers]
+    grad_act = joined_along(parts, 1)
     grad_up = (grad_act * silu_grad(upper)).astype(jnp.bfloat16)
     partial_grad = jnp.einsum("erf,edf->erd", grad_up, w_up, preferred_element_type=jnp.float32)
     grad_expert = lax.psum_scatter(

time: 783 us -> 780 us (level)
  starting transfers between devices: 26.1 us -> 87.4 us
  blocking collectives: 263 us -> 210 us
  waiting for transfers between devices: 363 us -> 326 us
  matrix products: 19.5 us -> 34.9 us
  local copies, waits for them, and re-layouts: 41.8 us -> 50.3 us
    ppermute x0 -> x15, waiting for transfers between devices: none -> 122 us  [local(): coming = held if hop_2 == peers - 1 else lax.ppermute(held, 'ctx', ahead_2)]
    reduce_scatter x1, waiting for transfers between devices: 132 us -> 42.4 us  [local(): lax.psum_scatter(lax.dot_general(columns, attn_heads, (((0,), (1,)), ((),...]
    all_gather x1 -> x0, waiting for transfers between devices: 59.1 us -> none  [local(): grad_all = lax.all_gather(grad_in, 'ctx', axis=1, tiled=True)]
    all_to_all x2 -> x0, blocking collectives: 50.8 us -> none  [the longest x1 30.3 us: local(): lax.all_to_all(sent_rows, 'exp', split_axis=0, concat_axis=2, tiled=True)]
    ppermute x0 -> x15, starting transfers between devices: none -> 31.5 us  [local(): coming = held if hop_2 == peers - 1 else lax.ppermute(held, 'ctx', ahead_2)]
    all_to_all x0 -> x2, starting transfers between devices: none -> 30.1 us  [the longest x1 15.4 us: local(): lax.all_to_all(grad_send, 'exp', split_axis=0, concat_axis=2, tiled=True)]
    all_gather x1, waiting for transfers between devices: 29.6 us -> 0.01 us  [local(): all_rows = lax.all_gather(expert_in, 'ctx', axis=1, tiled=True)]
    reduce_scatter x1, waiting for transfers between devices: 86.2 us -> 56.7 us  [local(): lax.psum_scatter(partial_grad.astype(jnp.bfloat16), 'ctx', scatter_dimens...]
  transfers between devices with their start and end apart: 7 -> 23, of which waited for: 5 -> 20; matrix products, arithmetic and copies ran while one was open for 8% -> 10% of each run, Pallas kernels for 0% -> 0%
where the time goes in v1:
time: 780 us; the launch traced here: 776 us
  waiting for transfers between devices  326 us (42%)
  blocking collectives  210 us (27%)
  starting transfers between devices  87.4 us (11%)
  other arithmetic  51.4 us (7%)
  local copies, waits for them, and re-layouts  50.3 us (6%)
  matrix products  34.9 us (4%)
  between operations  15 us (2%)
    ppermute x15, waiting for transfers between devices, local(): coming = held if hop_2 == peers - 1 else lax.ppermute(held, 'ctx', ahead_2)  122 us
    reduce_scatter x1, waiting for transfers between devices, local(): lax.psum_scatter(partial_out.astype(jnp.bfloat16), 'ctx', scatter_dimensi...  81.5 us
    reduce_scatter x1, waiting for transfers between devices, local(): lax.psum_scatter(partial_grad.astype(jnp.bfloat16), 'ctx', scatter_dimens...  56.7 us
    all_gather x2, blocking collectives, prefix(): lax.all_gather(a.astype(kind), axis)  49.5 us
    psum x1, blocking collectives, local(): square_sum = lax.psum(jnp.sum(residual_f * residual_f, axis=1), 'exp')  46.1 us
    psum x1, blocking collectives, local(): inner_dot = lax.psum(jnp.sum(grad_normed * residual_f, axis=1), 'exp')  43.9 us
    reduce_scatter x1, waiting for transfers between devices, local(): lax.psum_scatter(lax.dot_general(columns, attn_heads, (((0,), (1,)), ((),...  42.4 us
    unnamed x1, blocking collectives  38.1 us
  transfers between devices with their start and end apart: 23, of which 20 were waited for; matrix products, arithmetic and copies ran while one was open for 10% of the time, Pallas kernels for 0%

profile of v1, /device:TPU:32, one launch (start us, length us, event | category | flops | bytes accessed | tf_op | source)
XLA Modules:
  0.0 775.6 jit_solution(16939186865032570426)
XLA Ops:
  11.4 26.3 %all-gather = bf16[2048,128]{1,0:T(8,128)(2,1)} all-gather(bf16[128,128]{1,0:T(8,128)(2,1)S(1)} %convolution_convert_fusion.5), channel_id=2, replica_groups=mesh['ctx'=16,'exp'=32] {'ctx'}, dimensions={0}, use_global_device_ids=true | all-gather | bytes 557056 | tf_op jit(solution)/shard_map/all_gather | solution.py:20
  39.7 38.1 %all-reduce = bf16[16]{0:T(256)(128)(2,1)S(1)} all-reduce(bf16[16]{0:T(256)(128)(2,1)S(1)} %dynamic-update-slice), channel_id=1, replica_groups=mesh['ctx'=16,'exp'=32] {'ctx'}, use_global_device_ids=true, to_apply=%add | all-reduce | flops 16 | bytes 64
  82.6 2.3 copy.125
  87.9 15.4 %all-to-all-start.2 = ((bf16[32,16,96]{2,1,0:T(8,128)(2,1)}), bf16[32,16,96]{2,1,0:T(8,128)(2,1)S(1)}, u32[]{:S(2)}, u32[]{:S(2)}) async-start(bf16[32,16,96]{2,1,0:T(8,128)(2,1)} %bitcast.29), calls=%async_computation.3 | async-start | bytes 262144 | tf_op jit(solution)/shard_map/all_to_all | solution.py:159
  103.3 15.7 %all-to-all-done.2 = bf16[32,16,96]{2,1,0:T(8,128)(2,1)S(1)} async-done(((bf16[32,16,96]{2,1,0:T(8,128)(2,1)}), bf16[32,16,96]{2,1,0:T(8,128)(2,1)S(1)}, u32[]{:S(2)}, u32[]{:S(2)}) %all-to-all-start.2) | async-done | bytes 98336 | tf_op jit(solution)/shard_map/all_to_all | solution.py:159
  119.4 3.3 collective-permute-start
  123.4 31.3 %collective-permute-done = bf16[1,16,3072]{2,1,0:T(8,128)(2,1)S(1)} collective-permute-done((bf16[1,16,3072]{2,1,0:T(8,128)(2,1)S(1)}, bf16[1,16,3072]{2,1,0:T(8,128)(2,1)S(1)}, u32[]{:S(2)}, u32[]{:S(2)}) %collective-permute-start) | collective-permute-done | bytes 98336 | tf_op jit(solution)/shard_map/ppermute | solution.py:165
  154.8 1.9 collective-permute-start.1
  157.4 7.2 collective-permute-done.1
  164.6 1.9 collective-permute-start.2
  167.2 7.2 collective-permute-done.2
  174.4 1.9 collective-permute-start.3
  176.3 42.4 %reduce-scatter.10.cloned.1.call-done = bf16[96,128]{1,0:T(8,128)(2,1)} async-done(((bf16[3072,128]{1,0:T(8,128)(2,1)}), bf16[96,128]{1,0:T(8,128)(2,1)}) %reduce-scatter.10.cloned.1.call-update) | async-done | bytes 24592 | tf_op jit(solution)/shard_map/reduce_scatter | solution.py:102
  219.5 46.1 %psum.14 = f32[128]{0:T(128)S(1)} all-reduce(f32[128]{0:T(128)S(1)} %get-tuple-element.215), channel_id=1, replica_groups=mesh['ctx'=16,'exp'=32] {'exp'}, use_global_device_ids=true, to_apply=%region_9.10 | all-reduce | flops 128 | bytes 1024 | tf_op jit(solution)/shard_map/psum | solution.py:115
  266.5 14.7 %all-to-all-start = ((bf16[32,16,96]{2,1,0:T(8,128)(2,1)}), bf16[32,16,96]{2,1,0:T(8,128)(2,1)S(1)}, u32[]{:S(2)}, u32[]{:S(2)}) async-start(bf16[32,16,96]{2,1,0:T(8,128)(2,1)} %bitcast.16), calls=%async_computation | async-start | bytes 262144 | tf_op jit(solution)/shard_map/all_to_all | solution.py:132
  281.9 3.2 collective-permute-start.4
  285.1 1.6 fusion.80
  286.7 5.8 collective-permute-done.4
  292.5 1.9 collective-permute-start.5
  294.4 2.5 all-to-all-done
  298.6 3.9 collective-permute-done.5
  302.5 1.9 collective-permute-start.6
  304.4 1.6 fusion.92
  306.0 6.5 collective-permute-done.6
  312.5 1.9 collective-permute-start.7
  315.1 7.5 collective-permute-done.7
  322.6 1.9 collective-permute-start.8
  325.2 7.2 collective-permute-done.8
  332.4 1.9 collective-permute-start.9
  335.0 7.2 collective-permute-done.9
  342.2 1.9 collective-permute-start.10
  344.8 8.8 %collective-permute-done.10 = bf16[1,16,3072]{2,1,0:T(8,128)(2,1)S(1)} collective-permute-done((bf16[1,16,3072]{2,1,0:T(8,128)(2,1)S(1)}, bf16[1,16,3072]{2,1,0:T(8,128)(2,1)S(1)}, u32[]{:S(2)}, u32[]{:S(2)}) %collective-permute-start.10) | collective-permute-done | bytes 98336 | tf_op jit(solution)/shard_map/ppermute | solution.py:165
  353.6 1.9 collective-permute-start.11
  356.2 7.8 %collective-permute-done.11 = bf16[1,16,3072]{2,1,0:T(8,128)(2,1)S(1)} collective-permute-done((bf16[1,16,3072]{2,1,0:T(8,128)(2,1)S(1)}, bf16[1,16,3072]{2,1,0:T(8,128)(2,1)S(1)}, u32[]{:S(2)}, u32[]{:S(2)}) %collective-permute-start.11) | collective-permute-done | bytes 98336 | tf_op jit(solution)/shard_map/ppermute | solution.py:165
  364.0 1.9 collective-permute-start.12
  366.6 7.6 collective-permute-done.12
  374.2 2.1 collective-permute-start.13
  377.0 7.0 collective-permute-done.13
  384.0 1.9 collective-permute-start.14
  386.6 7.2 collective-permute-done.14
  394.5 1.3 gather_fusion
  395.9 3.2 fusion.150
  399.1 2.2 fusion
  401.4 3.8 fusion.1
  405.2 81.5 %reduce-scatter.6.cloned.1.call-done = bf16[1,16,3072]{2,1,0:T(8,128)(2,1)} async-done(((bf16[1,256,3072]{2,1,0:T(8,128)(2,1)}), bf16[1,16,3072]{2,1,0:T(8,128)(2,1)}) %reduce-scatter.6.cloned.1.call-update) | async-done | bytes 98320 | tf_op jit(solution)/shard_map/reduce_scatter | solution.py:137
  486.8 3.6 copy.106
  490.9 18.0 %reduce.3 = bf16[3072,16]{1,0:T(8,128)(2,1)S(1)} reduce(bf16[3072,1,16]{2,1,0:T(2,128)(2,1)} %bitcast.371, bf16[]{:T(256)} %broadcast.139), dimensions={1}, to_apply=%bitcast.325.reduce_sub_computation | reduce | bytes 196610
  510.2 12.9 %all-to-all-start.1 = ((bf16[32,2,768]{2,1,0:T(2,128)(2,1)}), bf16[32,2,768]{2,1,0:T(2,128)(2,1)}, u32[]{:S(2)}, u32[]{:S(2)}) async-start(bf16[32,2,768]{2,1,0:T(2,128)(2,1)} %reshape.440), calls=%async_computation.2 | async-start | bytes 196608 | tf_op jit(solution)/shard_map/all_to_all | solution.py:140
  523.1 56.7 %reduce-scatter.8.cloned.1.call-done = bf16[1,16,3072]{2,1,0:T(8,128)(2,1)} async-done(((bf16[1,256,3072]{2,1,0:T(8,128)(2,1)}), bf16[1,16,3072]{2,1,0:T(8,128)(2,1)}) %reduce-scatter.8.cloned.1.call-update) | async-done | bytes 98320 | tf_op jit(solution)/shard_map/reduce_scatter | solution.py:172
  579.7 3.6 copy.113
  583.3 18.0 %reduce.2 = bf16[3072,16]{1,0:T(8,128)(2,1)S(1)} reduce(bf16[3072,1,16]{2,1,0:T(2,128)(2,1)} %bitcast.372, bf16[]{:T(256)} %broadcast.139), dimensions={1}, to_apply=%bitcast.327.reduce_sub_computation | reduce | bytes 196610
  602.6 12.9 %all-to-all-start.3 = ((bf16[32,2,768]{2,1,0:T(2,128)(2,1)}), bf16[32,2,768]{2,1,0:T(2,128)(2,1)}, u32[]{:S(2)}, u32[]{:S(2)}) async-start(bf16[32,2,768]{2,1,0:T(2,128)(2,1)} %reshape.442), calls=%async_computation.5 | async-start | bytes 196608 | tf_op jit(solution)/shard_map/all_to_all | solution.py:175
  615.5 4.9 reshape.441
  620.4 3.3 copy.107
  624.9 5.2 all-to-all-done.3
  630.1 4.9 reshape.443
  635.0 3.9 copy.114
  639.0 1.7 all_to_all.60
  642.5 43.9 %psum.15 = f32[128]{0:T(128)S(1)} all-reduce(f32[128]{0:T(128)S(1)} %get-tuple-element.223), channel_id=1, replica_groups=mesh['ctx'=16,'exp'=32] {'exp'}, use_global_device_ids=true, to_apply=%region_14.15 | all-reduce | flops 128 | bytes 1024 | tf_op jit(solution)/shard_map/psum | solution.py:179
  687.1 1.5 fusion.183
  689.1 32.3 %all_gather.28 = bf16[128,3072]{0,1:T(8,128)(2,1)S(1)} all-gather(bf16[128,96]{0,1:T(8,128)(2,1)S(1)} %get-tuple-element.217), channel_id=1, replica_groups=mesh['ctx'=16,'exp'=32] {'exp'}, dimensions={1}, use_global_device_ids=true | all-gather | bytes 811008 | tf_op jit(solution)/shard_map/all_gather | solution.py:186
  723.2 23.2 %all-gather.1 = bf16[2048,128]{1,0:T(8,128)(2,1)S(1)} all-gather(bf16[128,128]{1,0:T(8,128)(2,1)S(1)} %convolution_convert_fusion.4), channel_id=3, replica_groups=mesh['ctx'=16,'exp'=32] {'ctx'}, dimensions={0}, use_global_device_ids=true | all-gather | bytes 557056 | tf_op jit(solution)/shard_map/all_gather | solution.py:20
  746.5 19.2 %while.27 = (s32[]{:T(128)}, f32[1,128,128]{2,1,0:T(8,128)S(1)}, s32[]{:T(128)}, bf16[16,1,128,128]{3,2,1,0:T(8,128)(2,1)S(1)}, bf16[16,1]{0,1:T(2,128)(2,1)S(1)...) while((s32[]{:T(128)}, f32[1,128,128]{2,1,0:T(8,128)S(1)}, s32[]{:T(128)}, ...), condition=%wide.region_16.17_spmd, body=%wide.region_15.16_spmd.sunk | while | flops 49158 | bytes 163997 | solution.py:35
  765.7 1.6 fusion.52
  (147 shorter events, 55.7 us)
Async XLA Ops:
  7.2 115.5 %copy-start = (bf16[1,384,3072]{2,1,0:T(8,128)(2,1)S(1)}, bf16[1,384,3072]{2,1,0:T(8,128)(2,1)}, u32[]{:S(2)}) copy-start(bf16[1,384,3072]{2,1,0:T(8,128)(2,1)} %param.22) | copy-start | bytes 7077892
  7.2 74.1 %copy-start.1 = (bf16[128,3072]{1,0:T(8,128)(2,1)S(1)}, bf16[128,3072]{1,0:T(8,128)(2,1)}, u32[]{:S(2)}) copy-start(bf16[128,3072]{1,0:T(8,128)(2,1)} %param.20) | copy-start | bytes 2359300
  7.2 211.5 %reduce-scatter.10.cloned.1.call-start = ((), (), s32[]{:S(2)}) async-start(), calls=%async_computation.10 | async-start | bytes 811008 | tf_op jit(solution)/shard_map/reduce_scatter | solution.py:102
  77.8 7.1 copy-start.14
  77.8 7.1 copy-start.12
  78.8 0.6 copy-start.7
  80.3 6.1 copy-start.13
  81.3 5.6 copy-start.10
  87.9 31.1 %all-to-all-start.2 = ((bf16[32,16,96]{2,1,0:T(8,128)(2,1)}), bf16[32,16,96]{2,1,0:T(8,128)(2,1)S(1)}, u32[]{:S(2)}, u32[]{:S(2)}) async-start(bf16[32,16,96]{2,1,0:T(8,128)(2,1)} %bitcast.29), calls=%async_computation.3 | async-start | bytes 262144 | tf_op jit(solution)/shard_map/all_to_all | solution.py:159
  119.4 35.4 %collective-permute-start = (bf16[1,16,3072]{2,1,0:T(8,128)(2,1)S(1)}, bf16[1,16,3072]{2,1,0:T(8,128)(2,1)S(1)}, u32[]{:S(2)}, u32[]{:S(2)}) collective-permute-start(bf16[1,16,3072]{2,1,0:T(8,128)(2,1)S(1)} %all_to_all.58), channel_id=1, source_target_pairs={{0,32},{32,64},{64,96},{96,128},{128,160},{160,192},{192,224},{224... | collective-permute-start | bytes 294920 | tf_op jit(solution)/shard_map/ppermute | solution.py:165
  123.4 95.3 %copy-start.11 = (bf16[128,96]{0,1:T(8,128)(2,1)S(1)}, bf16[128,96]{0,1:T(8,128)(2,1)}, u32[]{:S(2)}) copy-start(bf16[128,96]{0,1:T(8,128)(2,1)} %param.15) | copy-start | bytes 73732
  154.8 9.8 %collective-permute-start.1 = (bf16[1,16,3072]{2,1,0:T(8,128)(2,1)S(1)}, bf16[1,16,3072]{2,1,0:T(8,128)(2,1)S(1)}, u32[]{:S(2)}, u32[]{:S(2)}) collective-permute-start(bf16[1,16,3072]{2,1,0:T(8,128)(2,1)S(1)} %collective-permute-done), channel_id=1, source_target_pairs={{0,32},{32,64},{64,96},{96,128},{128,160},{160,192},{192,224},{224... | collective-permute-start | bytes 294920 | tf_op jit(solution)/shard_map/ppermute | solution.py:165
  164.6 9.8 %collective-permute-start.2 = (bf16[1,16,3072]{2,1,0:T(8,128)(2,1)S(1)}, bf16[1,16,3072]{2,1,0:T(8,128)(2,1)S(1)}, u32[]{:S(2)}, u32[]{:S(2)}) collective-permute-start(bf16[1,16,3072]{2,1,0:T(8,128)(2,1)S(1)} %collective-permute-done.1), channel_id=1, source_target_pairs={{0,32},{32,64},{64,96},{96,128},{128,160},{160,192},{192,224},{224... | collective-permute-start | bytes 294920 | tf_op jit(solution)/shard_map/ppermute | solution.py:165
  174.4 107.5 %collective-permute-start.3 = (bf16[1,16,3072]{2,1,0:T(8,128)(2,1)S(1)}, bf16[1,16,3072]{2,1,0:T(8,128)(2,1)}, u32[]{:S(2)}, u32[]{:S(2)}) collective-permute-start(bf16[1,16,3072]{2,1,0:T(8,128)(2,1)S(1)} %collective-permute-done.2), channel_id=1, source_target_pairs={{0,32},{32,64},{64,96},{96,128},{128,160},{160,192},{192,224},{224... | collective-permute-start | bytes 294920 | tf_op jit(solution)/shard_map/ppermute | solution.py:165
  265.5 21.2 %copy-start.16 = (f32[128]{0:T(128)}, f32[128]{0:T(128)S(1)}, u32[]{:S(2)}) copy-start(f32[128]{0:T(128)S(1)} %psum.14) | copy-start | bytes 1540
  266.5 30.5 %all-to-all-start = ((bf16[32,16,96]{2,1,0:T(8,128)(2,1)}), bf16[32,16,96]{2,1,0:T(8,128)(2,1)S(1)}, u32[]{:S(2)}, u32[]{:S(2)}) async-start(bf16[32,16,96]{2,1,0:T(8,128)(2,1)} %bitcast.16), calls=%async_computation | async-start | bytes 262144 | tf_op jit(solution)/shard_map/all_to_all | solution.py:132
  281.2 114.7 %all-gather.4.cloned.1.call-start = ((), (), s32[]{:S(2)}) async-start(), calls=%async_computation.7 | async-start | bytes 1671168 | tf_op jit(solution)/shard_map/all_gather | solution.py:133
  281.9 10.6 %collective-permute-start.4 = (bf16[1,16,3072]{2,1,0:T(8,128)(2,1)}, bf16[1,16,3072]{2,1,0:T(8,128)(2,1)S(1)}, u32[]{:S(2)}, u32[]{:S(2)}) collective-permute-start(bf16[1,16,3072]{2,1,0:T(8,128)(2,1)} %collective-permute-done.3), channel_id=1, source_target_pairs={{0,32},{32,64},{64,96},{96,128},{128,160},{160,192},{192,224},{224... | collective-permute-start | bytes 294920 | tf_op jit(solution)/shard_map/ppermute | solution.py:165
  292.5 9.9 %collective-permute-start.5 = (bf16[1,16,3072]{2,1,0:T(8,128)(2,1)S(1)}, bf16[1,16,3072]{2,1,0:T(8,128)(2,1)}, u32[]{:S(2)}, u32[]{:S(2)}) collective-permute-start(bf16[1,16,3072]{2,1,0:T(8,128)(2,1)S(1)} %collective-permute-done.4), channel_id=1, source_target_pairs={{0,32},{32,64},{64,96},{96,128},{128,160},{160,192},{192,224},{224... | collective-permute-start | bytes 294920 | tf_op jit(solution)/shard_map/ppermute | solution.py:165
  297.8 188.9 %reduce-scatter.6.cloned.1.call-start = ((), (), s32[]{:S(2)}) async-start(), calls=%async_computation.8 | async-start | bytes 1671168 | tf_op jit(solution)/shard_map/reduce_scatter | solution.py:137
  302.5 10.0 %collective-permute-start.6 = (bf16[1,16,3072]{2,1,0:T(8,128)(2,1)}, bf16[1,16,3072]{2,1,0:T(8,128)(2,1)S(1)}, u32[]{:S(2)}, u32[]{:S(2)}) collective-permute-start(bf16[1,16,3072]{2,1,0:T(8,128)(2,1)} %collective-permute-done.5), channel_id=1, source_target_pairs={{0,32},{32,64},{64,96},{96,128},{128,160},{160,192},{192,224},{224... | collective-permute-start | bytes 294920 | tf_op jit(solution)/shard_map/ppermute | solution.py:165
  312.5 10.1 %collective-permute-start.7 = (bf16[1,16,3072]{2,1,0:T(8,128)(2,1)S(1)}, bf16[1,16,3072]{2,1,0:T(8,128)(2,1)S(1)}, u32[]{:S(2)}, u32[]{:S(2)}) collective-permute-start(bf16[1,16,3072]{2,1,0:T(8,128)(2,1)S(1)} %collective-permute-done.6), channel_id=1, source_target_pairs={{0,32},{32,64},{64,96},{96,128},{128,160},{160,192},{192,224},{224... | collective-permute-start | bytes 294920 | tf_op jit(solution)/shard_map/ppermute | solution.py:165
  322.6 9.8 %collective-permute-start.8 = (bf16[1,16,3072]{2,1,0:T(8,128)(2,1)S(1)}, bf16[1,16,3072]{2,1,0:T(8,128)(2,1)S(1)}, u32[]{:S(2)}, u32[]{:S(2)}) collective-permute-start(bf16[1,16,3072]{2,1,0:T(8,128)(2,1)S(1)} %collective-permute-done.7), channel_id=1, source_target_pairs={{0,32},{32,64},{64,96},{96,128},{128,160},{160,192},{192,224},{224... | collective-permute-start | bytes 294920 | tf_op jit(solution)/shard_map/ppermute | solution.py:165
  332.4 9.8 %collective-permute-start.9 = (bf16[1,16,3072]{2,1,0:T(8,128)(2,1)S(1)}, bf16[1,16,3072]{2,1,0:T(8,128)(2,1)S(1)}, u32[]{:S(2)}, u32[]{:S(2)}) collective-permute-start(bf16[1,16,3072]{2,1,0:T(8,128)(2,1)S(1)} %collective-permute-done.8), channel_id=1, source_target_pairs={{0,32},{32,64},{64,96},{96,128},{128,160},{160,192},{192,224},{224... | collective-permute-start | bytes 294920 | tf_op jit(solution)/shard_map/ppermute | solution.py:165
  342.2 11.4 %collective-permute-start.10 = (bf16[1,16,3072]{2,1,0:T(8,128)(2,1)S(1)}, bf16[1,16,3072]{2,1,0:T(8,128)(2,1)S(1)}, u32[]{:S(2)}, u32[]{:S(2)}) collective-permute-start(bf16[1,16,3072]{2,1,0:T(8,128)(2,1)S(1)} %collective-permute-done.9), channel_id=1, source_target_pairs={{0,32},{32,64},{64,96},{96,128},{128,160},{160,192},{192,224},{224... | collective-permute-start | bytes 294920 | tf_op jit(solution)/shard_map/ppermute | solution.py:165
  353.6 10.4 %collective-permute-start.11 = (bf16[1,16,3072]{2,1,0:T(8,128)(2,1)S(1)}, bf16[1,16,3072]{2,1,0:T(8,128)(2,1)S(1)}, u32[]{:S(2)}, u32[]{:S(2)}) collective-permute-start(bf16[1,16,3072]{2,1,0:T(8,128)(2,1)S(1)} %collective-permute-done.10), channel_id=1, source_target_pairs={{0,32},{32,64},{64,96},{96,128},{128,160},{160,192},{192,224},{224... | collective-permute-start | bytes 294920 | tf_op jit(solution)/shard_map/ppermute | solution.py:165
  364.0 10.2 %collective-permute-start.12 = (bf16[1,16,3072]{2,1,0:T(8,128)(2,1)S(1)}, bf16[1,16,3072]{2,1,0:T(8,128)(2,1)S(1)}, u32[]{:S(2)}, u32[]{:S(2)}) collective-permute-start(bf16[1,16,3072]{2,1,0:T(8,128)(2,1)S(1)} %collective-permute-done.11), channel_id=1, source_target_pairs={{0,32},{32,64},{64,96},{96,128},{128,160},{160,192},{192,224},{224... | collective-permute-start | bytes 294920 | tf_op jit(solution)/shard_map/ppermute | solution.py:165
  374.2 9.8 %collective-permute-start.13 = (bf16[1,16,3072]{2,1,0:T(8,128)(2,1)S(1)}, bf16[1,16,3072]{2,1,0:T(8,128)(2,1)S(1)}, u32[]{:S(2)}, u32[]{:S(2)}) collective-permute-start(bf16[1,16,3072]{2,1,0:T(8,128)(2,1)S(1)} %collective-permute-done.12), channel_id=1, source_target_pairs={{0,32},{32,64},{64,96},{96,128},{128,160},{160,192},{192,224},{224... | collective-permute-start | bytes 294920 | tf_op jit(solution)/shard_map/ppermute | solution.py:165
  384.0 9.8 %collective-permute-start.14 = (bf16[1,16,3072]{2,1,0:T(8,128)(2,1)S(1)}, bf16[1,16,3072]{2,1,0:T(8,128)(2,1)S(1)}, u32[]{:S(2)}, u32[]{:S(2)}) collective-permute-start(bf16[1,16,3072]{2,1,0:T(8,128)(2,1)S(1)} %collective-permute-done.13), channel_id=1, source_target_pairs={{0,32},{32,64},{64,96},{96,128},{128,160},{160,192},{192,224},{224... | collective-permute-start | bytes 294920 | tf_op jit(solution)/shard_map/ppermute | solution.py:165
  401.3 178.4 %reduce-scatter.8.cloned.1.call-start = ((), (), s32[]{:S(2)}) async-start(), calls=%async_computation.9 | async-start | bytes 1671168 | tf_op jit(solution)/shard_map/reduce_scatter | solution.py:172
  510.2 92.4 %all-to-all-start.1 = ((bf16[32,2,768]{2,1,0:T(2,128)(2,1)}), bf16[32,2,768]{2,1,0:T(2,128)(2,1)}, u32[]{:S(2)}, u32[]{:S(2)}) async-start(bf16[32,2,768]{2,1,0:T(2,128)(2,1)} %reshape.440), calls=%async_computation.2 | async-start | bytes 196608 | tf_op jit(solution)/shard_map/all_to_all | solution.py:140
  602.6 27.5 %all-to-all-start.3 = ((bf16[32,2,768]{2,1,0:T(2,128)(2,1)}), bf16[32,2,768]{2,1,0:T(2,128)(2,1)}, u32[]{:S(2)}, u32[]{:S(2)}) async-start(bf16[32,2,768]{2,1,0:T(2,128)(2,1)} %reshape.442), calls=%async_computation.5 | async-start | bytes 196608 | tf_op jit(solution)/shard_map/all_to_all | solution.py:175
  624.9 96.6 %copy-start.2 = (bf16[128,3072]{1,0:T(8,128)(2,1)S(1)}, bf16[128,3072]{1,0:T(8,128)(2,1)}, u32[]{:S(2)}) copy-start(bf16[128,3072]{1,0:T(8,128)(2,1)} %param.20) | copy-start | bytes 2359300
  639.0 83.6 %copy-start.3 = (bf16[128,128]{1,0:T(8,128)(2,1)S(1)}, bf16[128,128]{1,0:T(8,128)(2,1)}, u32[]{:S(2)}) copy-start(bf16[128,128]{1,0:T(8,128)(2,1)} %param.18) | copy-start | bytes 98308
  640.7 105.8 %copy-start.15 = (bf16[16,1]{0,1:T(2,128)(2,1)S(1)}, bf16[16,1]{0,1:T(2,128)(2,1)}, u32[]{:S(2)}) copy-start(bf16[16,1]{0,1:T(2,128)(2,1)} %copy-done.14) | copy-start | bytes 100
  642.5 79.4 %copy-start.6 = (bf16[128,128]{1,0:T(8,128)(2,1)S(1)}, bf16[128,128]{1,0:T(8,128)(2,1)}, u32[]{:S(2)}) copy-start(bf16[128,128]{1,0:T(8,128)(2,1)} %param.16) | copy-start | bytes 98308
  642.5 79.8 %copy-start.8 = (f32[128,128]{1,0:T(8,128)S(1)}, f32[128,128]{1,0:T(8,128)}, u32[]{:S(2)}) copy-start(f32[128,128]{1,0:T(8,128)} %copy-done.7) | copy-start | bytes 196612
  642.5 80.5 %copy-start.5 = (bf16[128,128]{1,0:T(8,128)(2,1)S(1)}, bf16[128,128]{1,0:T(8,128)(2,1)}, u32[]{:S(2)}) copy-start(bf16[128,128]{1,0:T(8,128)(2,1)} %param.17) | copy-start | bytes 98308
  688.5 0.6 copy-start.9
  721.9 45.4 %copy-start.4 = (bf16[128,128]{1,0:T(8,128)(2,1)S(1)}, bf16[128,128]{1,0:T(8,128)(2,1)}, u32[]{:S(2)}) copy-start(bf16[128,128]{1,0:T(8,128)(2,1)} %param.18) | copy-start | bytes 98308
Sparse Core Ops, SparseCore 0:
  85.0 133.6 reduce-scatter.9
  297.9 60.0 all-gather.3
  401.4 85.2 reduce-scatter.5
  491.3 88.4 reduce-scatter.7
